TPU v7x, 32 devices: a whole 2x2x4 slice. The times are simulated.
32 devices in a mesh: cube: 8 (over y, x, core), grid: 4 (over z).
Axes of the slice: x: 2, y: 2, z: 4, core: 2. Of those that a mesh axis runs over, the one named last changes fastest.
Arguments:
- child_update: bfloat16 [512, 2048], P('cube', 'grid'), may hold values from -6 to 6
- child_panel: bfloat16 [512, 512], P('grid', 'cube'), may hold values from -6 to 6
- panel_entries: bfloat16 [512, 4096], P('grid', 'cube'), may hold values from -6 to 6
- panel_inverse: bfloat16 [512, 512], replicated, as said below
- block_owner: int32 [128], replicated, may hold values from 0 to 7, as said below
- child_dest: int32 [32], replicated, may hold values from 0 to 127, as said below
- child_rows: int32 [32, 16], P('cube'), may hold values from 0 to 15, each once within a row
Outputs:
- schur_update: bfloat16 [4096, 2048], P('cube', 'grid')
- panel_factor: bfloat16 [512, 4096], P('grid', 'cube')
Inputs may be any that keep to these rules, and one draw needn't show every extreme that they name: `block_owner`: row blocks r*32 to (r+1)*32 - 1 form column range r. One cube index owns at most 8 row blocks of one range, and in every draw some cube index owns exactly 8 of some range. Every cube index owns at least one row block. `child_dest`: entry s*4+k names the parent row block into which child row block k of cube index s adds. The 4 child row blocks of one cube index go to blocks of 4 different owners, and in every draw some owner receives a block from every cube index. `panel_inverse`: zero below the diagonal, positive on it.
All inputs are finite; a program needn't handle non-finite values.
Results may differ from a plain program's by a relative error of at most 0.0057.
Values may be sent and summed in bfloat16 or wider, within the bound.
No kernel may reach another device: no remote copies, remote signals or barrier semaphores. Data moves between devices by JAX's collectives and lax.ppermute only.
A program may use at most 64 MiB of HBM per device.

v0:
```python
import functools

import jax
import jax.numpy as jnp
from jax import lax
from jax.experimental import pallas as pl
from jax.experimental.pallas import tpu as pltpu
from jax.sharding import PartitionSpec as P

F32 = jnp.float32
BF16 = jnp.bfloat16
I32 = jnp.int32
VMEM = pl.BlockSpec(memory_space=pltpu.VMEM)
SMEM = pl.BlockSpec(memory_space=pltpu.SMEM)
ANY = pl.BlockSpec(memory_space=pl.ANY)
MIB = 1024 * 1024
PACK_COST = 1500000000


def call(body, outs, in_specs, scratch, flops, moved, out_specs=None, limit=16, aliases={}):
    return pl.pallas_call(
        body,
        out_shape=outs,
        in_specs=in_specs,
        out_specs=[VMEM] * len(outs) if out_specs is None else out_specs,
        scratch_shapes=scratch,
        input_output_aliases=aliases,
        compiler_params=pltpu.CompilerParams(vmem_limit_bytes=limit * MIB),
        cost_estimate=pl.CostEstimate(flops=flops, bytes_accessed=moved, transcendentals=0),
    )


def rows_at(index, size):
    return pl.ds(pl.multiple_of(index * size, size), size)


def prepare_body(
    cubes, grids, span, owner_hbm, dest_hbm, rows_hbm, update_hbm, panel_hbm, entries_hbm, inverse_hbm, *refs
):
    firsts, rests, blocks_ref, turned_ref = refs[:grids], refs[grids : 2 * grids - 1], *refs[2 * grids - 1 : 2 * grids + 1]
    owner_ref, dest_ref, rows_ref, update_ref, panel_ref, entries_ref, flipped, sems = refs[2 * grids + 1 :]
    copies = [
        pltpu.make_async_copy(source, target, sems.at[i])
        for i, (source, target) in enumerate(
            (
                (entries_hbm, entries_ref),
                (panel_hbm, panel_ref),
                (rows_hbm, rows_ref),
                (update_hbm, update_ref),
                (owner_hbm, owner_ref),
                (dest_hbm, dest_ref),
            )
        )
    ]
    mine = lax.axis_index("cube")
    column = lax.axis_index("grid")
    depth = entries_ref.shape[0]
    for d in range(grids):
        part = inverse_hbm.at[rows_at(jnp.bitwise_xor(column, d), depth), :]
        copies.append(pltpu.make_async_copy(part, turned_ref.at[pl.ds(d * depth, depth), :], sems.at[6 + d]))
    for copy in copies:
        copy.start()
    children, rows = rows_ref.shape
    base = span + children * rows
    blocks_ref[...] = jnp.zeros_like(blocks_ref)
    copies[0].wait()
    flipped[...] = entries_ref[...].astype(F32).T.astype(BF16)
    for d in range(grids):
        piece = flipped[rows_at(jnp.bitwise_xor(column, d), span), :]
        firsts[d][pl.ds(0, span), :] = piece
        for e in range(grids):
            if e != d:
                k = d if d < e else d - 1
                if e == 1:
                    firsts[1][pl.ds(base + k * span, span), :] = piece
                else:
                    rests[max(e - 1, 0)][pl.ds(k * span, span), :] = piece
    for copy in copies[1:6]:
        copy.wait()
    for k in range(children):
        want = rows_ref[k : k + 1, :]
        put = (lax.broadcasted_iota(I32, (rows, rows), 0) == want).astype(BF16)
        part = pl.ds(k * rows, rows)
        placed = jnp.dot(put, panel_ref[part, :], preferred_element_type=F32).astype(BF16)
        for d in range(grids):
            firsts[d][pl.ds(span + k * rows, rows), :] = placed
        moved = jnp.dot(put, update_ref[part, :], preferred_element_type=F32).astype(BF16)
        d = jnp.bitwise_xor(owner_ref[dest_ref[mine * children + k]], mine)
        blocks_ref[rows_at(d, rows), :] = moved
    for copy in copies[6:]:
        copy.wait()


def pack_body(parts, rows, base, blocks_ref, *refs):
    firsts, payloads = refs[: len(parts)], refs[len(parts) :]
    depth = firsts[0].shape[1]
    panel = payloads[0].shape[1]
    chunks = blocks_ref.shape[1] // panel
    for d, first in zip(parts, firsts):
        piece = first[...]
        for payload in payloads:
            payload[pl.ds(0, base), pl.ds(d * depth, depth)] = piece
    for i, payload in enumerate(payloads):
        for half in range(2):
            for j in range(chunks):
                at = base + (half * chunks + j) * rows
                block = blocks_ref[pl.ds((2 * i + half) * rows, rows), pl.ds(j * panel, panel)]
                payload[pl.ds(at, rows), :] = block


def complete_body(base, plan_ref, first_ref, *refs):
    depth = first_ref.shape[1]
    piece = first_ref[pl.ds(0, base), :]
    for payload in refs[len(refs) // 2 :]:
        payload[pl.ds(0, base), pl.ds(depth, depth)] = piece


def plan_body(cubes, grids, slots, owner_hbm, dest_hbm, out_ref, owner_ref, dest_ref, slot_ref, count_ref, sems):
    fetches = [
        pltpu.make_async_copy(owner_hbm, owner_ref, sems.at[0]),
        pltpu.make_async_copy(dest_hbm, dest_ref, sems.at[1]),
    ]
    for fetch in fetches:
        fetch.start()
    for fetch in fetches:
        fetch.wait()
    mine = lax.axis_index("cube")
    column = lax.axis_index("grid")
    blocks = owner_ref.shape[0]
    in_range = blocks // grids
    children = dest_ref.shape[0] // cubes
    none = grids * slots
    places = 2 * cubes + grids
    child_places = places + cubes * slots
    for r in range(grids):

        def count_own(i, seen):
            b = r * in_range + i
            own = owner_ref[b] == mine
            slot_ref[b] = jnp.where(own, r * slots + seen, none)
            return seen + own.astype(I32)

        out_ref[2 * cubes + r] = lax.fori_loop(0, in_range, count_own, I32(0), unroll=8)
    for d in range(cubes):
        source = jnp.bitwise_xor(mine, d)
        slot, which = I32(none), I32(0)
        for k in range(children):
            b = dest_ref[source * children + k]
            here = slot_ref[b]
            which = jnp.where(here < none, k, which)
            slot = jnp.minimum(slot, here)
            local_b = b - column * in_range
            inside = jnp.logical_and(local_b >= 0, local_b < in_range)
            out_ref[child_places + d * children + k] = jnp.where(inside, local_b, in_range)
        out_ref[d] = slot
        out_ref[cubes + d] = which
        count_ref[d] = 0
        for k in range(slots):
            out_ref[places + d * slots + k] = in_range

    def place(i, carry):
        d = jnp.bitwise_xor(owner_ref[column * in_range + i], mine)
        k = count_ref[d]
        out_ref[places + d * slots + k] = i
        count_ref[d] = k + 1
        return carry

    lax.fori_loop(0, in_range, place, 0, unroll=8)


def own_body(cubes, grids, span, rows, base, plan_ref, turned_ref, mine_ref, full_ref, *refs):
    rests = refs[: grids - 1]
    entries_ref, factor_ref = refs[grids - 1 :]
    column = lax.axis_index("grid")
    depth = rests[0].shape[1]
    for e in range(grids):
        r = jnp.bitwise_xor(column, e)
        ids = lax.broadcasted_iota(I32, (span, depth), 0)
        live = ids < plan_ref[2 * cubes + r] * rows
        for d in range(grids):
            if e == 0:
                piece = mine_ref[pl.ds(0, span), pl.ds(d * depth, depth)]
            else:
                k = d ^ e
                at = (k if k < d else k - 1) * span
                if d == 1:
                    piece = full_ref[pl.ds(base + at, span), :]
                else:
                    piece = rests[max(d - 1, 0)][pl.ds(at, span), :]
            piece = jnp.where(live, piece.astype(F32), 0.0).astype(BF16)
            entries_ref[rows_at(r, span), pl.ds(d * depth, depth)] = piece
    factor_ref[...] = jnp.dot(entries_ref[...], turned_ref[...], preferred_element_type=F32).astype(BF16)


def join_body(*refs):
    pass


def add_children(cubes, grids, slots, rows, children, plan_ref, pieces, ranged, touched, total):
    span = slots * rows
    base = span + children * rows
    panel = ranged.shape[1]
    chunks = total.shape[1] // panel
    child_places = 2 * cubes + grids + cubes * slots
    in_range = ranged.shape[0] // rows - 1
    for d, piece in pieces.items():
        at = rows_at(plan_ref[d], rows)
        touched[at, :] += piece[rows_at(slots + plan_ref[cubes + d], rows), :].astype(F32)
        for j in range(chunks):
            part = pl.ds(base + ((d & 1) * chunks + j) * rows, rows)
            total[at, pl.ds(j * panel, panel)] += piece[part, :].astype(F32)
        for k in range(children):
            place = plan_ref[child_places + d * children + k]

            @pl.when(place < in_range)
            def _():
                ranged[rows_at(place, rows), :] += piece[pl.ds(span + k * rows, rows), :].astype(F32)


def early_body(cubes, grids, slots, rows, children, plan_ref, entries_ref, *refs):
    pieces = dict(enumerate(refs[:-3]))
    ranged, touched, total = refs[-3:]
    places = 2 * cubes + grids
    none = entries_ref.shape[0] // rows
    ranged[...] = jnp.zeros_like(ranged)
    total[...] = jnp.zeros_like(total)
    for d in range(cubes):
        slot = plan_ref[d]
        touched[rows_at(slot, rows), :] = entries_ref[rows_at(jnp.minimum(slot, none - 1), rows), :].astype(F32)
    for d, piece in pieces.items():
        for k in range(slots):
            at = rows_at(plan_ref[places + d * slots + k], rows)
            ranged[at, :] = piece[pl.ds(k * rows, rows), :].astype(F32)
    add_children(cubes, grids, slots, rows, children, plan_ref, pieces, ranged, touched, total)


def schur_body(cubes, grids, slots, rows, children, plan_ref, turned_ref, before_ref, *refs):
    pieces = {cubes - 2: refs[0], cubes - 1: refs[1]}
    out_ref, panel_ref, ranged, touched, total, few, factor_ref = refs[5:]
    column = lax.axis_index("grid")
    own_rows, width = out_ref.shape
    depth = panel_ref.shape[0]
    places = 2 * cubes + grids
    in_range = width // rows
    for d, piece in pieces.items():
        for k in range(slots):
            place = plan_ref[places + d * slots + k]

            @pl.when(place < in_range)
            def _():
                ranged[rows_at(place, rows), :] += piece[pl.ds(k * rows, rows), :].astype(F32)

    add_children(cubes, grids, slots, rows, children, plan_ref, pieces, ranged, touched, total)
    for d in range(cubes):
        few[pl.ds(d * rows, rows), :] = touched[rows_at(plan_ref[d], rows), :].astype(BF16)
    redone = jnp.dot(few[...], turned_ref[...], preferred_element_type=F32).astype(BF16)
    factor_ref[pl.ds(0, own_rows), :] = before_ref[...]
    for d in range(cubes):
        factor_ref[rows_at(plan_ref[d], rows), :] = redone[d * rows : (d + 1) * rows, :]
    column_factor = jnp.dot(
        ranged[pl.ds(0, width), :].astype(BF16), turned_ref[...], preferred_element_type=F32
    ).astype(BF16)
    product = lax.dot_general(
        factor_ref[pl.ds(0, own_rows), :], column_factor, (((1,), (1,)), ((), ())), preferred_element_type=F32
    )
    out_ref[...] = (total[pl.ds(0, own_rows), :] - product).astype(BF16)
    if depth % 128 == 0:
        cols = pl.ds(pl.multiple_of(column * depth, depth), depth)
        panel_ref[...] = factor_ref[pl.ds(0, own_rows), cols].astype(F32).T.astype(BF16)
    else:
        for r in range(grids):

            @pl.when(column == r)
            def _():
                part = factor_ref[pl.ds(0, own_rows), pl.ds(r * depth, depth)]
                panel_ref[...] = part.astype(F32).T.astype(BF16)


def local(
    child_update, child_panel, panel_entries, panel_inverse, block_owner, child_dest, child_rows
):
    cubes = lax.axis_size("cube")
    grids = lax.axis_size("grid")
    chips = cubes // 2
    children, rows = child_rows.shape
    width = child_update.shape[1]
    depth = child_panel.shape[0]
    panel = panel_inverse.shape[0]
    own_rows = panel_entries.shape[1]
    slots = own_rows // rows // grids
    span = slots * rows
    base = span + children * rows
    sent = base + 2 * rows * (width // panel)
    like = jax.ShapeDtypeStruct
    small = own_rows * width <= 512 * 512
    kept = pltpu.VMEM if small else like

    def in_hbm(x):
        return pltpu.with_memory_space_constraint(x, pltpu.HBM)

    def join(first, *others):
        if small:
            first, *others = (
                pltpu.with_memory_space_constraint(x, pltpu.SMEM if x.dtype == I32 else pltpu.VMEM)
                for x in (first, *others)
            )
        return pl.pallas_call(
            join_body,
            out_shape=kept(first.shape, first.dtype),
            in_specs=[ANY] * (1 + len(others)),
            out_specs=ANY,
            input_output_aliases={0: 0},
        )(first, *others)

    def swap(x, axis, d):
        n = lax.axis_size(axis)
        return lax.ppermute(x, axis, [(i, i ^ d) for i in range(n)])

    rest_rows = (grids - 1) * span
    prepared = call(
        functools.partial(prepare_body, cubes, grids, span),
        [kept((base + (rest_rows if d == 1 else 0), depth), BF16) for d in range(grids)]
        + [kept((rest_rows, depth), BF16)] * (grids - 1)
        + [kept((cubes * rows, width), BF16), kept((panel, panel), BF16)],
        [ANY] * 7,
        [
            pltpu.SMEM(block_owner.shape, I32),
            pltpu.SMEM(child_dest.shape, I32),
            pltpu.VMEM(child_rows.shape, I32),
            pltpu.VMEM(child_update.shape, BF16),
            pltpu.VMEM(child_panel.shape[::-1], BF16),
            pltpu.VMEM(panel_entries.shape, BF16),
            pltpu.VMEM(panel_entries.shape[::-1], BF16),
            pltpu.SemaphoreType.DMA((6 + grids,)),
        ],
        2 * rows * rows * children * (width + depth),
        4 * own_rows * depth,
        limit=28,
    )(*(in_hbm(x) for x in (block_owner, child_dest, child_rows, child_update, child_panel.T, panel_entries, panel_inverse)))
    firsts, rests = list(prepared[:grids]), list(prepared[grids:-2])
    blocks, turned = prepared[-2:]
    for d in [*range(2, grids), 1]:
        firsts[d] = swap(firsts[d], "grid", d)
    plan = call(
        functools.partial(plan_body, cubes, grids, slots),
        [pltpu.SMEM((2 * cubes + grids + cubes * (slots + children),), I32)],
        [ANY, ANY],
        [
            pltpu.SMEM(block_owner.shape, I32),
            pltpu.SMEM(child_dest.shape, I32),
            pltpu.SMEM(block_owner.shape, I32),
            pltpu.SMEM((cubes,), I32),
            pltpu.SemaphoreType.DMA((2,)),
        ],
        100000,
        6000000,
        [SMEM],
    )(in_hbm(block_owner), in_hbm(child_dest))[0]
    for d in range(2, grids):
        rests[d - 1] = swap(join(rests[d - 1], plan), "grid", d)
    plan = pltpu.with_memory_space_constraint(plan, pltpu.SMEM)
    parts = [*range(2, grids), 0]
    packed = call(
        functools.partial(pack_body, parts, rows, base),
        [kept((sent, panel), BF16)] * chips,
        [VMEM] * (1 + len(parts)),
        [],
        PACK_COST,
        2 * chips * sent * panel,
    )(blocks, *(firsts[d] for d in parts))
    packed = call(
        functools.partial(complete_body, base),
        [kept((sent, panel), BF16)] * chips,
        [ANY] + [VMEM] * (1 + chips),
        [],
        1000,
        2 * chips * base * depth,
        aliases={2 + i: i for i in range(chips)},
    )(plan, firsts[1], *packed)
    arrived = [packed[0]] + [swap(packed[i], "cube", 2 * i) for i in range(1, chips)]
    entries, before = call(
        functools.partial(own_body, cubes, grids, span, rows, base),
        [kept((own_rows, panel), BF16), kept((own_rows, panel), BF16)],
        [SMEM] + [VMEM] * (2 + grids),
        [],
        1650000000,
        2 * own_rows * panel * panel,
    )(plan, turned, packed[0], firsts[1], *rests)
    arrived[1] = join(arrived[1], before)
    pieces = []
    for piece in arrived:
        pieces += [piece, swap(piece, "cube", 1)]
    sizes = (cubes, grids, slots, rows, children)
    shapes = [(width + rows, panel), (own_rows + rows, panel), (own_rows + rows, width)]
    early = call(
        functools.partial(early_body, *sizes),
        [kept(shape, F32) for shape in shapes],
        [SMEM] + [VMEM] * (cubes - 1),
        [],
        1000,
        4 * width * panel,
        limit=16 if small else 56,
    )(plan, entries, *pieces[:-2])
    return tuple(
        call(
            functools.partial(schur_body, *sizes),
            [like((own_rows, width), BF16), like((depth, own_rows), BF16)] + [kept(shape, F32) for shape in shapes],
            [SMEM] + [VMEM] * 7,
            [pltpu.VMEM((cubes * rows, panel), BF16), pltpu.VMEM((own_rows + rows, panel), BF16)],
            2 * own_rows * width * panel,
            2 * (own_rows * width + (own_rows + cubes * span) * panel),
            limit=16 if small else 56,
            aliases={5: 2, 6: 3, 7: 4},
        )(plan, turned, before, *pieces[-2:], *early)[:2]
    )


def solution(mesh):
    placed = (
        P("cube", "grid"),
        P("grid", "cube"),
        P("grid", "cube"),
        P(),
        P(),
        P(),
        P("cube", None),
    )
    return jax.shard_map(
        local,
        mesh=mesh,
        in_specs=placed,
        out_specs=(P("cube", "grid"), P("grid", "cube")),
        check_vma=False,
    )
```

profile of v0, /device:TPU:0, one launch (start us, length us, event | category | flops | bytes accessed | tf_op | source)
XLA Modules:
  0.0 29.3 jit_solution(15642674436679762057)
XLA Ops:
  0.6 1.4 %shard_map.87 = (bf16[192,128]{1,0:T(8,128)(2,1)S(1)}, bf16[576,128]{1,0:T(8,128)(2,1)S(1)}, bf16[192,128]{1,0:T(8,128)(2,1)S(1)}, bf16[192,128]{1,0:T(8,128)(2,...) custom-call(s32[128]{0:T(128)} %owner_hbm.3, ...), custom_call_target="tpu_custom_call" | custom-call | flops 1310720 | bytes 262144 | tf_op jit(solution)/shard_map/pallas_call | solution.py:320
  2.0 4.1 %collective-permute-start.1 = (bf16[192,128]{1,0:T(8,128)(2,1)S(1)}, bf16[192,128]{1,0:T(8,128)(2,1)S(1)}, u32[]{:S(2)}, u32[]{:S(2)}) collective-permute-start(bf16[192,128]{1,0:T(8,128)(2,1)S(1)} %get-tuple-element.29), channel_id=1, source_target_pairs={{0,2},{1,3},{2,0},{3,1},{4,6},{5,7},{6,4},{7,5},{8,10},{9,11},{10,... | collective-permute-start | bytes 147464 | tf_op jit(solution)/shard_map/ppermute | solution.py:317
  6.1 1.4 %collective-permute-start.2 = (bf16[192,128]{1,0:T(8,128)(2,1)S(1)}, bf16[192,128]{1,0:T(8,128)(2,1)S(1)}, u32[]{:S(2)}, u32[]{:S(2)}) collective-permute-start(bf16[192,128]{1,0:T(8,128)(2,1)S(1)} %get-tuple-element.30), channel_id=1, source_target_pairs={{0,3},{1,2},{2,1},{3,0},{4,7},{5,6},{6,5},{7,4},{8,11},{9,10},{10,... | collective-permute-start | bytes 147464 | tf_op jit(solution)/shard_map/ppermute | solution.py:317
  7.5 0.2 collective-permute-start
  7.7 1.4 %shard_map.86.plan_ref.refs_1_ = s32[116]{0:T(128)S(4)} custom-call(s32[128]{0:T(128)} %owner_hbm.3, s32[32]{0:T(128)} %dest_hbm.3), custom_call_target="tpu_custom_call" | custom-call | flops 100000 | bytes 6000000 | tf_op jit(solution)/shard_map/pallas_call | solution.py:344
  9.1 3.0 %collective-permute-start.4 = (bf16[384,128]{1,0:T(8,128)(2,1)S(1)}, bf16[384,128]{1,0:T(8,128)(2,1)S(1)}, u32[]{:S(2)}, u32[]{:S(2)}) collective-permute-start(bf16[384,128]{1,0:T(8,128)(2,1)S(1)} %shard_map.91), channel_id=1, source_target_pairs={{0,3},{1,2},{2,1},{3,0},{4,7},{5,6},{6,5},{7,4},{8,11},{9,10},{10,... | collective-permute-start | bytes 294920 | tf_op jit(solution)/shard_map/ppermute | solution.py:317
  12.1 0.3 %collective-permute-start.3 = (bf16[384,128]{1,0:T(8,128)(2,1)S(1)}, bf16[384,128]{1,0:T(8,128)(2,1)S(1)}, u32[]{:S(2)}, u32[]{:S(2)}) collective-permute-start(bf16[384,128]{1,0:T(8,128)(2,1)S(1)} %shard_map.90), channel_id=1, source_target_pairs={{0,2},{1,3},{2,0},{3,1},{4,6},{5,7},{6,4},{7,5},{8,10},{9,11},{10,... | collective-permute-start | bytes 294920 | tf_op jit(solution)/shard_map/ppermute | solution.py:317
  12.5 0.1 collective-permute-done.2.refs_1_
  12.6 0.1 shard_map.88
  12.7 1.5 %collective-permute-done.first_ref.full_ref = bf16[576,128]{1,0:T(8,128)(2,1)S(1)} collective-permute-done((bf16[576,128]{1,0:T(8,128)(2,1)S(1)}, bf16[576,128]{1,0:T(8,128)(2,1)S(1)}, u32[]{:S(2)}, u32[]{:S(2)}) %collective-permute-start) | collective-permute-done | bytes 147488 | tf_op jit(solution)/shard_map/ppermute | solution.py:317
  14.2 1.6 %collective-permute-start.10 = (bf16[224,512]{1,0:T(8,128)(2,1)S(1)}, bf16[224,512]{1,0:T(8,128)(2,1)S(1)}, u32[]{:S(2)}, u32[]{:S(2)}) collective-permute-start(bf16[224,512]{1,0:T(8,128)(2,1)S(1)} %get-tuple-element.44), channel_id=1, source_target_pairs={{0,16},{4,20},{8,24},{12,28},{16,0},{20,4},{24,8},{28,12},{1,17},{... | collective-permute-start | bytes 688136 | tf_op jit(solution)/shard_map/ppermute | solution.py:317
  15.8 1.5 %collective-permute-start.8 = (bf16[224,512]{1,0:T(8,128)(2,1)S(1)}, bf16[224,512]{1,0:T(8,128)(2,1)S(1)}, u32[]{:S(2)}, u32[]{:S(2)}) collective-permute-start(bf16[224,512]{1,0:T(8,128)(2,1)S(1)} %get-tuple-element.43), channel_id=1, source_target_pairs={{0,8},{4,12},{8,0},{12,4},{16,24},{20,28},{24,16},{28,20},{1,9},{5... | collective-permute-start | bytes 688136 | tf_op jit(solution)/shard_map/ppermute | solution.py:317
  17.3 0.5 %collective-permute-start.5 = (bf16[224,512]{1,0:T(8,128)(2,1)S(1)}, bf16[224,512]{1,0:T(8,128)(2,1)S(1)}, u32[]{:S(2)}, u32[]{:S(2)}) collective-permute-start(bf16[224,512]{1,0:T(8,128)(2,1)S(1)} %get-tuple-element.41), channel_id=1, source_target_pairs={{0,24},{4,28},{8,16},{12,20},{16,8},{20,12},{24,0},{28,4},{1,25},{... | collective-permute-start | bytes 688136 | tf_op jit(solution)/shard_map/ppermute | solution.py:317
  17.8 0.0 collective-permute-done.4.refs_2_
  17.8 0.0 collective-permute-start.7
  17.8 3.0 %collective-permute-done.3.refs_1_ = bf16[384,128]{1,0:T(8,128)(2,1)S(1)} collective-permute-done((bf16[384,128]{1,0:T(8,128)(2,1)S(1)}, bf16[384,128]{1,0:T(8,128)(2,1)S(1)}, u32[]{:S(2)}, u32[]{:S(2)}) %collective-permute-start.3) | collective-permute-done | bytes 98336 | tf_op jit(solution)/shard_map/ppermute | solution.py:317
  20.8 0.5 %shard_map.92 = (bf16[512,512]{1,0:T(8,128)(2,1)S(1)}, bf16[512,512]{1,0:T(8,128)(2,1)S(1)}) custom-call(s32[116]{0:T(128)S(4)} %shard_map.86.plan_ref.refs_1_, bf16[512,512]{1,0:T(8,128)(2,1)S(1)} %get-tuple-element.26.turned_ref, bf16[224,512]{1,0:T(8,128)(2,1)S(1)} %get-tuple-element.36.mine_ref.refs_0_, ...), custom_call_target="tpu_custom_call" | custom-call | flops 1650000000 | bytes 268435456 | tf_op jit(solution)/shard_map/pallas_call | solution.py:381
  21.4 1.4 %collective-permute-done.10.refs_4_ = bf16[224,512]{1,0:T(8,128)(2,1)S(1)} collective-permute-done((bf16[224,512]{1,0:T(8,128)(2,1)S(1)}, bf16[224,512]{1,0:T(8,128)(2,1)S(1)}, u32[]{:S(2)}, u32[]{:S(2)}) %collective-permute-start.10) | collective-permute-done | bytes 229408 | tf_op jit(solution)/shard_map/ppermute | solution.py:317
  22.8 0.0 collective-permute-start.11
  22.8 0.7 %collective-permute-done.8.refs_0_ = bf16[224,512]{1,0:T(8,128)(2,1)S(1)} collective-permute-done((bf16[224,512]{1,0:T(8,128)(2,1)S(1)}, bf16[224,512]{1,0:T(8,128)(2,1)S(1)}, u32[]{:S(2)}, u32[]{:S(2)}) %collective-permute-start.8) | collective-permute-done | bytes 229408 | tf_op jit(solution)/shard_map/ppermute | solution.py:317
  23.5 2.4 %collective-permute-done.5.refs_0_ = bf16[224,512]{1,0:T(8,128)(2,1)S(1)} collective-permute-done((bf16[224,512]{1,0:T(8,128)(2,1)S(1)}, bf16[224,512]{1,0:T(8,128)(2,1)S(1)}, u32[]{:S(2)}, u32[]{:S(2)}) %collective-permute-start.5) | collective-permute-done | bytes 229408 | tf_op jit(solution)/shard_map/ppermute | solution.py:317
  25.9 0.5 %shard_map.94 = (f32[528,512]{1,0:T(8,128)S(1)}, f32[528,512]{1,0:T(8,128)S(1)}, f32[528,512]{1,0:T(8,128)S(1)}) custom-call(s32[116]{0:T(128)S(4)} %shard_map.86.plan_ref.refs_1_, bf16[512,512]{1,0:T(8,128)(2,1)S(1)} %get-tuple-element.42.entries_ref, bf16[224,512]{1,0:T(8,128)(2,1)S(1)} %get-tuple-element.36.mine_ref.refs_0_, ...), custom_call_target="tpu_custom_call" | custom-call | flops 1000 | bytes 1048576 | tf_op jit(solution)/shard_map/pallas_call | solution.py:395
  26.4 0.9 %collective-permute-done.6.refs_1_ = bf16[224,512]{1,0:T(8,128)(2,1)S(1)} collective-permute-done((bf16[224,512]{1,0:T(8,128)(2,1)S(1)}, bf16[224,512]{1,0:T(8,128)(2,1)S(1)}, u32[]{:S(2)}, u32[]{:S(2)}) %collective-permute-start.6) | collective-permute-done | bytes 229408 | tf_op jit(solution)/shard_map/ppermute | solution.py:317
  27.4 1.9 %shard_map.95 = (bf16[512,512]{1,0:T(8,128)(2,1)}, bf16[128,512]{1,0:T(8,128)(2,1)}, f32[528,512]{1,0:T(8,128)S(1)}, f32[528,512]{1,0:T(8,128)S(1)}, f32[528,512]{1,0:T(8,128)S(1)}) custom-call(s32[116]{0:T(128)S(4)} %shard_map.86.plan_ref.refs_1_, ...), custom_call_target="tpu_custom_call", output_to_operand_aliasing={{2}: (5, {}), {3}: (6, {}), {4}: (7, {})} | custom-call | flops 268435456 | bytes 2097152 | tf_op jit(solution)/shard_map/pallas_call | solution.py:405
  (10 shorter events, 0.0 us)
Async XLA Ops:
  2.0 10.5 %collective-permute-start.1 = (bf16[192,128]{1,0:T(8,128)(2,1)S(1)}, bf16[192,128]{1,0:T(8,128)(2,1)S(1)}, u32[]{:S(2)}, u32[]{:S(2)}) collective-permute-start(bf16[192,128]{1,0:T(8,128)(2,1)S(1)} %get-tuple-element.29), channel_id=1, source_target_pairs={{0,2},{1,3},{2,0},{3,1},{4,6},{5,7},{6,4},{7,5},{8,10},{9,11},{10,... | collective-permute-start | bytes 147464 | tf_op jit(solution)/shard_map/ppermute | solution.py:317
  6.1 6.5 %collective-permute-start.2 = (bf16[192,128]{1,0:T(8,128)(2,1)S(1)}, bf16[192,128]{1,0:T(8,128)(2,1)S(1)}, u32[]{:S(2)}, u32[]{:S(2)}) collective-permute-start(bf16[192,128]{1,0:T(8,128)(2,1)S(1)} %get-tuple-element.30), channel_id=1, source_target_pairs={{0,3},{1,2},{2,1},{3,0},{4,7},{5,6},{6,5},{7,4},{8,11},{9,10},{10,... | collective-permute-start | bytes 147464 | tf_op jit(solution)/shard_map/ppermute | solution.py:317
  7.5 6.7 %collective-permute-start = (bf16[576,128]{1,0:T(8,128)(2,1)S(1)}, bf16[576,128]{1,0:T(8,128)(2,1)S(1)}, u32[]{:S(2)}, u32[]{:S(2)}) collective-permute-start(bf16[576,128]{1,0:T(8,128)(2,1)S(1)} %get-tuple-element.27), channel_id=1, source_target_pairs={{0,1},{1,0},{2,3},{3,2},{4,5},{5,4},{6,7},{7,6},{8,9},{9,8},{10,11... | collective-permute-start | bytes 442376 | tf_op jit(solution)/shard_map/ppermute | solution.py:317
  9.1 8.7 %collective-permute-start.4 = (bf16[384,128]{1,0:T(8,128)(2,1)S(1)}, bf16[384,128]{1,0:T(8,128)(2,1)S(1)}, u32[]{:S(2)}, u32[]{:S(2)}) collective-permute-start(bf16[384,128]{1,0:T(8,128)(2,1)S(1)} %shard_map.91), channel_id=1, source_target_pairs={{0,3},{1,2},{2,1},{3,0},{4,7},{5,6},{6,5},{7,4},{8,11},{9,10},{10,... | collective-permute-start | bytes 294920 | tf_op jit(solution)/shard_map/ppermute | solution.py:317
  12.1 8.7 %collective-permute-start.3 = (bf16[384,128]{1,0:T(8,128)(2,1)S(1)}, bf16[384,128]{1,0:T(8,128)(2,1)S(1)}, u32[]{:S(2)}, u32[]{:S(2)}) collective-permute-start(bf16[384,128]{1,0:T(8,128)(2,1)S(1)} %shard_map.90), channel_id=1, source_target_pairs={{0,2},{1,3},{2,0},{3,1},{4,6},{5,7},{6,4},{7,5},{8,10},{9,11},{10,... | collective-permute-start | bytes 294920 | tf_op jit(solution)/shard_map/ppermute | solution.py:317
  14.2 8.5 %collective-permute-start.10 = (bf16[224,512]{1,0:T(8,128)(2,1)S(1)}, bf16[224,512]{1,0:T(8,128)(2,1)S(1)}, u32[]{:S(2)}, u32[]{:S(2)}) collective-permute-start(bf16[224,512]{1,0:T(8,128)(2,1)S(1)} %get-tuple-element.44), channel_id=1, source_target_pairs={{0,16},{4,20},{8,24},{12,28},{16,0},{20,4},{24,8},{28,12},{1,17},{... | collective-permute-start | bytes 688136 | tf_op jit(solution)/shard_map/ppermute | solution.py:317
  15.8 7.7 %collective-permute-start.8 = (bf16[224,512]{1,0:T(8,128)(2,1)S(1)}, bf16[224,512]{1,0:T(8,128)(2,1)S(1)}, u32[]{:S(2)}, u32[]{:S(2)}) collective-permute-start(bf16[224,512]{1,0:T(8,128)(2,1)S(1)} %get-tuple-element.43), channel_id=1, source_target_pairs={{0,8},{4,12},{8,0},{12,4},{16,24},{20,28},{24,16},{28,20},{1,9},{5... | collective-permute-start | bytes 688136 | tf_op jit(solution)/shard_map/ppermute | solution.py:317
  17.3 8.6 %collective-permute-start.5 = (bf16[224,512]{1,0:T(8,128)(2,1)S(1)}, bf16[224,512]{1,0:T(8,128)(2,1)S(1)}, u32[]{:S(2)}, u32[]{:S(2)}) collective-permute-start(bf16[224,512]{1,0:T(8,128)(2,1)S(1)} %get-tuple-element.41), channel_id=1, source_target_pairs={{0,24},{4,28},{8,16},{12,20},{16,8},{20,12},{24,0},{28,4},{1,25},{... | collective-permute-start | bytes 688136 | tf_op jit(solution)/shard_map/ppermute | solution.py:317
  17.8 8.1 %collective-permute-start.7 = (bf16[224,512]{1,0:T(8,128)(2,1)S(1)}, bf16[224,512]{1,0:T(8,128)(2,1)S(1)}, u32[]{:S(2)}, u32[]{:S(2)}) collective-permute-start(bf16[224,512]{1,0:T(8,128)(2,1)S(1)} %get-tuple-element.36.mine_ref.refs_0_), channel_id=1, source_target_pairs={{0,4},{4,0},{8,12},{12,8},{16,20},{20,16},{24,28},{28,24},{1,5},{5... | collective-permute-start | bytes 688136 | tf_op jit(solution)/shard_map/ppermute | solution.py:317
  22.8 3.1 %collective-permute-start.11 = (bf16[224,512]{1,0:T(8,128)(2,1)S(1)}, bf16[224,512]{1,0:T(8,128)(2,1)S(1)}, u32[]{:S(2)}, u32[]{:S(2)}) collective-permute-start(bf16[224,512]{1,0:T(8,128)(2,1)S(1)} %collective-permute-done.10.refs_4_), channel_id=1, source_target_pairs={{0,4},{4,0},{8,12},{12,8},{16,20},{20,16},{24,28},{28,24},{1,5},{5... | collective-permute-start | bytes 688136 | tf_op jit(solution)/shard_map/ppermute | solution.py:317
  23.5 2.4 %collective-permute-start.9 = (bf16[224,512]{1,0:T(8,128)(2,1)S(1)}, bf16[224,512]{1,0:T(8,128)(2,1)S(1)}, u32[]{:S(2)}, u32[]{:S(2)}) collective-permute-start(bf16[224,512]{1,0:T(8,128)(2,1)S(1)} %shard_map.93.refs_2_), channel_id=1, source_target_pairs={{0,4},{4,0},{8,12},{12,8},{16,20},{20,16},{24,28},{28,24},{1,5},{5... | collective-permute-start | bytes 688136 | tf_op jit(solution)/shard_map/ppermute | solution.py:317
  25.9 1.5 %collective-permute-start.6 = (bf16[224,512]{1,0:T(8,128)(2,1)S(1)}, bf16[224,512]{1,0:T(8,128)(2,1)S(1)}, u32[]{:S(2)}, u32[]{:S(2)}) collective-permute-start(bf16[224,512]{1,0:T(8,128)(2,1)S(1)} %collective-permute-done.5.refs_0_), channel_id=1, source_target_pairs={{0,4},{4,0},{8,12},{12,8},{16,20},{20,16},{24,28},{28,24},{1,5},{5... | collective-permute-start | bytes 688136 | tf_op jit(solution)/shard_map/ppermute | solution.py:317
where the time goes:
time: 29.5 us; the launch traced here: 29.3 us
  starting transfers between devices  12.6 us (43%)
  waiting for transfers between devices  10.1 us (34%)
  Pallas kernels  5.92 us (20%)
  between operations  0.71 us (2%)
    ppermute x12, starting transfers between devices, swap(): return lax.ppermute(x, axis, [(i, i ^ d) for i in range(n)])  12.6 us
    ppermute x12, waiting for transfers between devices, swap(): return lax.ppermute(x, axis, [(i, i ^ d) for i in range(n)])  10.1 us
    pallas_call x1, Pallas kernels, local(): call(functools.partial(schur_body, *sizes), [like((own_rows, width), BF16...  1.94 us
    pallas_call x1, Pallas kernels, local(): call(functools.partial(plan_body, cubes, grids, slots), [pltpu.SMEM((2 *...  1.42 us
    pallas_call x1, Pallas kernels, local(): call(functools.partial(prepare_body, cubes, grids, span), [kept((base + (...  1.37 us
  transfers between devices with their start and end apart: 12, of which 7 were waited for; matrix products, arithmetic and copies ran while one was open for 0% of the time, Pallas kernels for 9%

commit v1 on v0

--- a/solution.py
+++ b/solution.py
@@ -14,7 +14,6 @@
 SMEM = pl.BlockSpec(memory_space=pltpu.SMEM)
 ANY = pl.BlockSpec(memory_space=pl.ANY)
 MIB = 1024 * 1024
-PACK_COST = 1500000000
 
 
 def call(body, outs, in_specs, scratch, flops, moved, out_specs=None, limit=16, aliases={}):
@@ -37,8 +36,8 @@
 def prepare_body(
     cubes, grids, span, owner_hbm, dest_hbm, rows_hbm, update_hbm, panel_hbm, entries_hbm, inverse_hbm, *refs
 ):
-    firsts, rests, blocks_ref, turned_ref = refs[:grids], refs[grids : 2 * grids - 1], *refs[2 * grids - 1 : 2 * grids + 1]
-    owner_ref, dest_ref, rows_ref, update_ref, panel_ref, entries_ref, flipped, sems = refs[2 * grids + 1 :]
+    firsts, rests, blocks_ref, turned_ref = refs[:grids], refs[grids : 2 * grids], *refs[2 * grids : 2 * grids + 2]
+    owner_ref, dest_ref, rows_ref, update_ref, panel_ref, entries_ref, flipped, sems = refs[2 * grids + 2 :]
     copies = [
         pltpu.make_async_copy(source, target, sems.at[i])
         for i, (source, target) in enumerate(
@@ -61,7 +60,6 @@
     for copy in copies:
         copy.start()
     children, rows = rows_ref.shape
-    base = span + children * rows
     blocks_ref[...] = jnp.zeros_like(blocks_ref)
     copies[0].wait()
     flipped[...] = entries_ref[...].astype(F32).T.astype(BF16)
@@ -71,10 +69,7 @@
         for e in range(grids):
             if e != d:
                 k = d if d < e else d - 1
-                if e == 1:
-                    firsts[1][pl.ds(base + k * span, span), :] = piece
-                else:
-                    rests[max(e - 1, 0)][pl.ds(k * span, span), :] = piece
+                rests[e][pl.ds(k * span, span), :] = piece
     for copy in copies[1:6]:
         copy.wait()
     for k in range(children):
@@ -106,13 +101,6 @@
                 at = base + (half * chunks + j) * rows
                 block = blocks_ref[pl.ds((2 * i + half) * rows, rows), pl.ds(j * panel, panel)]
                 payload[pl.ds(at, rows), :] = block
-
-
-def complete_body(base, plan_ref, first_ref, *refs):
-    depth = first_ref.shape[1]
-    piece = first_ref[pl.ds(0, base), :]
-    for payload in refs[len(refs) // 2 :]:
-        payload[pl.ds(0, base), pl.ds(depth, depth)] = piece
 
 
 def plan_body(cubes, grids, slots, owner_hbm, dest_hbm, out_ref, owner_ref, dest_ref, slot_ref, count_ref, sems):
@@ -168,9 +156,9 @@
     lax.fori_loop(0, in_range, place, 0, unroll=8)
 
 
-def own_body(cubes, grids, span, rows, base, plan_ref, turned_ref, mine_ref, full_ref, *refs):
-    rests = refs[: grids - 1]
-    entries_ref, factor_ref = refs[grids - 1 :]
+def own_body(cubes, grids, span, rows, plan_ref, turned_ref, mine_ref, *refs):
+    rests = refs[:grids]
+    entries_ref, factor_ref = refs[grids:]
     column = lax.axis_index("grid")
     depth = rests[0].shape[1]
     for e in range(grids):
@@ -183,13 +171,14 @@
             else:
                 k = d ^ e
                 at = (k if k < d else k - 1) * span
-                if d == 1:
-                    piece = full_ref[pl.ds(base + at, span), :]
-                else:
-                    piece = rests[max(d - 1, 0)][pl.ds(at, span), :]
+                piece = rests[d][pl.ds(at, span), :]
             piece = jnp.where(live, piece.astype(F32), 0.0).astype(BF16)
             entries_ref[rows_at(r, span), pl.ds(d * depth, depth)] = piece
     factor_ref[...] = jnp.dot(entries_ref[...], turned_ref[...], preferred_element_type=F32).astype(BF16)
+
+
+def marker_body(after_ref, out_ref):
+    out_ref[...] = jnp.zeros_like(out_ref)
 
 
 def join_body(*refs):
@@ -319,8 +308,8 @@
     rest_rows = (grids - 1) * span
     prepared = call(
         functools.partial(prepare_body, cubes, grids, span),
-        [kept((base + (rest_rows if d == 1 else 0), depth), BF16) for d in range(grids)]
-        + [kept((rest_rows, depth), BF16)] * (grids - 1)
+        [kept((base, depth), BF16)] * grids
+        + [kept((rest_rows, depth), BF16)] * grids
         + [kept((cubes * rows, width), BF16), kept((panel, panel), BF16)],
         [ANY] * 7,
         [
@@ -356,37 +345,30 @@
         6000000,
         [SMEM],
     )(in_hbm(block_owner), in_hbm(child_dest))[0]
+    marker = call(marker_body, [kept((8, 128), F32)], [VMEM], [], 1000, 0)(firsts[0])[0]
     for d in range(2, grids):
-        rests[d - 1] = swap(join(rests[d - 1], plan), "grid", d)
+        rests[d] = swap(join(rests[d], marker), "grid", d)
     plan = pltpu.with_memory_space_constraint(plan, pltpu.SMEM)
-    parts = [*range(2, grids), 0]
+    parts = [*range(2, grids), 0, 1]
     packed = call(
         functools.partial(pack_body, parts, rows, base),
         [kept((sent, panel), BF16)] * chips,
-        [VMEM] * (1 + len(parts)),
+        [VMEM] * (1 + grids),
         [],
-        PACK_COST,
+        1000,
         2 * chips * sent * panel,
     )(blocks, *(firsts[d] for d in parts))
-    packed = call(
-        functools.partial(complete_body, base),
-        [kept((sent, panel), BF16)] * chips,
-        [ANY] + [VMEM] * (1 + chips),
-        [],
-        1000,
-        2 * chips * base * depth,
-        aliases={2 + i: i for i in range(chips)},
-    )(plan, firsts[1], *packed)
     arrived = [packed[0]] + [swap(packed[i], "cube", 2 * i) for i in range(1, chips)]
+    rests[1] = swap(join(rests[1], packed[0]), "grid", 1)
     entries, before = call(
-        functools.partial(own_body, cubes, grids, span, rows, base),
+        functools.partial(own_body, cubes, grids, span, rows),
         [kept((own_rows, panel), BF16), kept((own_rows, panel), BF16)],
         [SMEM] + [VMEM] * (2 + grids),
         [],
-        1650000000,
+        2200000000,
         2 * own_rows * panel * panel,
-    )(plan, turned, packed[0], firsts[1], *rests)
-    arrived[1] = join(arrived[1], before)
+    )(plan, turned, packed[0], *rests)
+    arrived[-1] = join(arrived[-1], before)
     pieces = []
     for piece in arrived:
         pieces += [piece, swap(piece, "cube", 1)]

time: 29.5 us -> 32.3 us (1.095)
  waiting for transfers between devices: 10.1 us -> 3.14 us
  starting transfers between devices: 12.6 us -> 19.2 us
  local copies, waits for them, and re-layouts: 0 us -> 3.06 us
    ppermute x12 -> x13, waiting for transfers between devices: 10.1 us -> 3.14 us  [swap(): return lax.ppermute(x, axis, [(i, i ^ d) for i in range(n)])]
    ppermute x12 -> x13, starting transfers between devices: 12.6 us -> 19.2 us  [swap(): return lax.ppermute(x, axis, [(i, i ^ d) for i in range(n)])]
    unnamed x0 -> x8, local copies, waits for them, and re-layouts: none -> 3.06 us
  transfers between devices with their start and end apart: 12 -> 13, of which waited for: 7 -> 3; matrix products, arithmetic and copies ran while one was open for 0% -> 0% of each run, Pallas kernels for 9% -> 8%
where the time goes in v1:
time: 32.3 us; the launch traced here: 32 us
  starting transfers between devices  19.2 us (59%)
  Pallas kernels  5.94 us (18%)
  waiting for transfers between devices  3.14 us (10%)
  local copies, waits for them, and re-layouts  3.06 us (9%)
  between operations  0.73 us (2%)
    ppermute x13, starting transfers between devices, swap(): return lax.ppermute(x, axis, [(i, i ^ d) for i in range(n)])  19.2 us
    ppermute x13, waiting for transfers between devices, swap(): return lax.ppermute(x, axis, [(i, i ^ d) for i in range(n)])  3.14 us
    unnamed x8, local copies, waits for them, and re-layouts  3.06 us
    pallas_call x1, Pallas kernels, local(): call(functools.partial(schur_body, *sizes), [like((own_rows, width), BF16...  1.95 us
    pallas_call x1, Pallas kernels, local(): call(functools.partial(plan_body, cubes, grids, slots), [pltpu.SMEM((2 *...  1.42 us
    pallas_call x1, Pallas kernels, local(): call(functools.partial(prepare_body, cubes, grids, span), [kept((base, de...  1.37 us
  transfers between devices with their start and end apart: 13, of which 3 were waited for; matrix products, arithmetic and copies ran while one was open for 0% of the time, Pallas kernels for 8%

profile of v1, /device:TPU:0, one launch (start us, length us, event | category | flops | bytes accessed | tf_op | source)
XLA Modules:
  0.0 32.0 jit_solution(17038839436819404414)
XLA Ops:
  0.6 1.4 %shard_map.87 = (bf16[192,128]{1,0:T(8,128)(2,1)S(1)}, bf16[192,128]{1,0:T(8,128)(2,1)S(1)}, bf16[192,128]{1,0:T(8,128)(2,1)S(1)}, bf16[192,128]{1,0:T(8,128)(2,...) custom-call(s32[128]{0:T(128)} %owner_hbm.3, ...), custom_call_target="tpu_custom_call" | custom-call | flops 1310720 | bytes 262144 | tf_op jit(solution)/shard_map/pallas_call | solution.py:309
  2.0 4.1 %collective-permute-start = (bf16[192,128]{1,0:T(8,128)(2,1)S(1)}, bf16[192,128]{1,0:T(8,128)(2,1)S(1)}, u32[]{:S(2)}, u32[]{:S(2)}) collective-permute-start(bf16[192,128]{1,0:T(8,128)(2,1)S(1)} %get-tuple-element.25), channel_id=1, source_target_pairs={{0,2},{1,3},{2,0},{3,1},{4,6},{5,7},{6,4},{7,5},{8,10},{9,11},{10,... | collective-permute-start | bytes 147464 | tf_op jit(solution)/shard_map/ppermute | solution.py:306
  6.1 1.4 %collective-permute-start.1 = (bf16[192,128]{1,0:T(8,128)(2,1)S(1)}, bf16[192,128]{1,0:T(8,128)(2,1)S(1)}, u32[]{:S(2)}, u32[]{:S(2)}) collective-permute-start(bf16[192,128]{1,0:T(8,128)(2,1)S(1)} %get-tuple-element.26), channel_id=1, source_target_pairs={{0,3},{1,2},{2,1},{3,0},{4,7},{5,6},{6,5},{7,4},{8,11},{9,10},{10,... | collective-permute-start | bytes 147464 | tf_op jit(solution)/shard_map/ppermute | solution.py:306
  7.5 0.2 collective-permute-start.2
  7.7 2.8 %collective-permute-start.4 = (bf16[384,128]{1,0:T(8,128)(2,1)S(1)}, bf16[384,128]{1,0:T(8,128)(2,1)S(1)}, u32[]{:S(2)}, u32[]{:S(2)}) collective-permute-start(bf16[384,128]{1,0:T(8,128)(2,1)S(1)} %shard_map.91), channel_id=1, source_target_pairs={{0,2},{1,3},{2,0},{3,1},{4,6},{5,7},{6,4},{7,5},{8,10},{9,11},{10,... | collective-permute-start | bytes 294920 | tf_op jit(solution)/shard_map/ppermute | solution.py:306
  10.5 1.4 %collective-permute-start.5 = (bf16[384,128]{1,0:T(8,128)(2,1)S(1)}, bf16[384,128]{1,0:T(8,128)(2,1)S(1)}, u32[]{:S(2)}, u32[]{:S(2)}) collective-permute-start(bf16[384,128]{1,0:T(8,128)(2,1)S(1)} %shard_map.92), channel_id=1, source_target_pairs={{0,3},{1,2},{2,1},{3,0},{4,7},{5,6},{6,5},{7,4},{8,11},{9,10},{10,... | collective-permute-start | bytes 294920 | tf_op jit(solution)/shard_map/ppermute | solution.py:306
  11.9 0.8 %collective-permute-done.1.refs_1_ = bf16[192,128]{1,0:T(8,128)(2,1)S(1)} collective-permute-done((bf16[192,128]{1,0:T(8,128)(2,1)S(1)}, bf16[192,128]{1,0:T(8,128)(2,1)S(1)}, u32[]{:S(2)}, u32[]{:S(2)}) %collective-permute-start.1) | collective-permute-done | bytes 49184 | tf_op jit(solution)/shard_map/ppermute | solution.py:306
  12.6 0.1 shard_map.88
  12.8 2.9 %collective-permute-start.3 = (bf16[384,128]{1,0:T(8,128)(2,1)S(1)}, bf16[384,128]{1,0:T(8,128)(2,1)S(1)}, u32[]{:S(2)}, u32[]{:S(2)}) collective-permute-start(bf16[384,128]{1,0:T(8,128)(2,1)S(1)} %shard_map.89), channel_id=1, source_target_pairs={{0,1},{1,0},{2,3},{3,2},{4,5},{5,4},{6,7},{7,6},{8,9},{9,8},{10,11... | collective-permute-start | bytes 294920 | tf_op jit(solution)/shard_map/ppermute | solution.py:306
  15.6 1.5 %collective-permute-start.9 = (bf16[224,512]{1,0:T(8,128)(2,1)S(1)}, bf16[224,512]{1,0:T(8,128)(2,1)S(1)}, u32[]{:S(2)}, u32[]{:S(2)}) collective-permute-start(bf16[224,512]{1,0:T(8,128)(2,1)S(1)} %get-tuple-element.37), channel_id=1, source_target_pairs={{0,8},{4,12},{8,0},{12,4},{16,24},{20,28},{24,16},{28,20},{1,9},{5... | collective-permute-start | bytes 688136 | tf_op jit(solution)/shard_map/ppermute | solution.py:306
  17.1 1.5 %collective-permute-start.11 = (bf16[224,512]{1,0:T(8,128)(2,1)S(1)}, bf16[224,512]{1,0:T(8,128)(2,1)S(1)}, u32[]{:S(2)}, u32[]{:S(2)}) collective-permute-start(bf16[224,512]{1,0:T(8,128)(2,1)S(1)} %get-tuple-element.38), channel_id=1, source_target_pairs={{0,16},{4,20},{8,24},{12,28},{16,0},{20,4},{24,8},{28,12},{1,17},{... | collective-permute-start | bytes 688136 | tf_op jit(solution)/shard_map/ppermute | solution.py:306
  18.6 0.6 %copy-done = bf16[384,128]{1,0:T(8,128)(2,1)} copy-done((bf16[384,128]{1,0:T(8,128)(2,1)}, bf16[384,128]{1,0:T(8,128)(2,1)S(1)}, u32[]{:S(2)}) %copy-start) | copy-done | bytes 98328
  19.3 2.4 %collective-permute-start.6 = (bf16[224,512]{1,0:T(8,128)(2,1)S(1)}, bf16[224,512]{1,0:T(8,128)(2,1)S(1)}, u32[]{:S(2)}, u32[]{:S(2)}) collective-permute-start(bf16[224,512]{1,0:T(8,128)(2,1)S(1)} %get-tuple-element.35), channel_id=1, source_target_pairs={{0,24},{4,28},{8,16},{12,20},{16,8},{20,12},{24,0},{28,4},{1,25},{... | collective-permute-start | bytes 688136 | tf_op jit(solution)/shard_map/ppermute | solution.py:306
  21.7 1.4 %shard_map.86.plan_ref = s32[116]{0:T(128)S(4)} custom-call(s32[128]{0:T(128)} %owner_hbm.3, s32[32]{0:T(128)} %dest_hbm.3), custom_call_target="tpu_custom_call" | custom-call | flops 100000 | bytes 6000000 | tf_op jit(solution)/shard_map/pallas_call | solution.py:333
  23.1 0.6 %copy-done.2 = bf16[384,128]{1,0:T(8,128)(2,1)} copy-done((bf16[384,128]{1,0:T(8,128)(2,1)}, bf16[384,128]{1,0:T(8,128)(2,1)S(1)}, u32[]{:S(2)}) %copy-start.2) | copy-done | bytes 98328
  23.8 0.9 %copy-done.1 = bf16[384,128]{1,0:T(8,128)(2,1)S(1)} copy-done((bf16[384,128]{1,0:T(8,128)(2,1)S(1)}, bf16[384,128]{1,0:T(8,128)(2,1)}, u32[]{:S(2)}) %copy-start.1) | copy-done | bytes 98328
  24.6 0.9 %copy-done.3 = bf16[384,128]{1,0:T(8,128)(2,1)S(1)} copy-done((bf16[384,128]{1,0:T(8,128)(2,1)S(1)}, bf16[384,128]{1,0:T(8,128)(2,1)}, u32[]{:S(2)}) %copy-start.3) | copy-done | bytes 98328
  25.5 0.5 %shard_map.93 = (bf16[512,512]{1,0:T(8,128)(2,1)S(1)}, bf16[512,512]{1,0:T(8,128)(2,1)S(1)}) custom-call(s32[116]{0:T(128)S(4)} %shard_map.86.plan_ref, bf16[512,512]{1,0:T(8,128)(2,1)S(1)} %get-tuple-element.23.turned_ref, bf16[224,512]{1,0:T(8,128)(2,1)S(1)} %get-tuple-element.29.refs_1_.mine_ref.refs_0_, bf16[384,128]{1,0:T(8,128)(2,1)S(1)} %get-tuple-element.30.refs_0_, ...), custom_call_target="tpu_custom_call" | custom-call | flops 2200000000 | bytes 268435456 | tf_op jit(solution)/shard_map/pallas_call | solution.py:363
  26.1 0.6 %collective-permute-start.10 = (bf16[224,512]{1,0:T(8,128)(2,1)S(1)}, bf16[224,512]{1,0:T(8,128)(2,1)S(1)}, u32[]{:S(2)}, u32[]{:S(2)}) collective-permute-start(bf16[224,512]{1,0:T(8,128)(2,1)S(1)} %collective-permute-done.9.refs_2_), channel_id=1, source_target_pairs={{0,4},{4,0},{8,12},{12,8},{16,20},{20,16},{24,28},{28,24},{1,5},{5... | collective-permute-start | bytes 688136 | tf_op jit(solution)/shard_map/ppermute | solution.py:306
  26.7 1.4 %collective-permute-done.11.refs_4_ = bf16[224,512]{1,0:T(8,128)(2,1)S(1)} collective-permute-done((bf16[224,512]{1,0:T(8,128)(2,1)S(1)}, bf16[224,512]{1,0:T(8,128)(2,1)S(1)}, u32[]{:S(2)}, u32[]{:S(2)}) %collective-permute-start.11) | collective-permute-done | bytes 229408 | tf_op jit(solution)/shard_map/ppermute | solution.py:306
  28.1 0.5 %collective-permute-start.7 = (bf16[224,512]{1,0:T(8,128)(2,1)S(1)}, bf16[224,512]{1,0:T(8,128)(2,1)S(1)}, u32[]{:S(2)}, u32[]{:S(2)}) collective-permute-start(bf16[224,512]{1,0:T(8,128)(2,1)S(1)} %shard_map.94.refs_0_), channel_id=1, source_target_pairs={{0,4},{4,0},{8,12},{12,8},{16,20},{20,16},{24,28},{28,24},{1,5},{5... | collective-permute-start | bytes 688136 | tf_op jit(solution)/shard_map/ppermute | solution.py:306
  28.6 1.0 %collective-permute-done.12.refs_5_ = bf16[224,512]{1,0:T(8,128)(2,1)S(1)} collective-permute-done((bf16[224,512]{1,0:T(8,128)(2,1)S(1)}, bf16[224,512]{1,0:T(8,128)(2,1)S(1)}, u32[]{:S(2)}, u32[]{:S(2)}) %collective-permute-start.12) | collective-permute-done | bytes 229408 | tf_op jit(solution)/shard_map/ppermute | solution.py:306
  29.6 0.5 %shard_map.95 = (f32[528,512]{1,0:T(8,128)S(1)}, f32[528,512]{1,0:T(8,128)S(1)}, f32[528,512]{1,0:T(8,128)S(1)}) custom-call(s32[116]{0:T(128)S(4)} %shard_map.86.plan_ref, bf16[512,512]{1,0:T(8,128)(2,1)S(1)} %get-tuple-element.36.entries_ref, bf16[224,512]{1,0:T(8,128)(2,1)S(1)} %get-tuple-element.29.refs_1_.mine_ref.refs_0_, ...), custom_call_target="tpu_custom_call" | custom-call | flops 1000 | bytes 1048576 | tf_op jit(solution)/shard_map/pallas_call | solution.py:377
  30.1 1.9 %shard_map.96 = (bf16[512,512]{1,0:T(8,128)(2,1)}, bf16[128,512]{1,0:T(8,128)(2,1)}, f32[528,512]{1,0:T(8,128)S(1)}, f32[528,512]{1,0:T(8,128)S(1)}, f32[528,512]{1,0:T(8,128)S(1)}) custom-call(s32[116]{0:T(128)S(4)} %shard_map.86.plan_ref, ...), custom_call_target="tpu_custom_call", output_to_operand_aliasing={{2}: (5, {}), {3}: (6, {}), {4}: (7, {})} | custom-call | flops 268435456 | bytes 2097152 | tf_op jit(solution)/shard_map/pallas_call | solution.py:387
  (21 shorter events, 0.0 us)
Async XLA Ops:
  2.0 9.9 %collective-permute-start = (bf16[192,128]{1,0:T(8,128)(2,1)S(1)}, bf16[192,128]{1,0:T(8,128)(2,1)S(1)}, u32[]{:S(2)}, u32[]{:S(2)}) collective-permute-start(bf16[192,128]{1,0:T(8,128)(2,1)S(1)} %get-tuple-element.25), channel_id=1, source_target_pairs={{0,2},{1,3},{2,0},{3,1},{4,6},{5,7},{6,4},{7,5},{8,10},{9,11},{10,... | collective-permute-start | bytes 147464 | tf_op jit(solution)/shard_map/ppermute | solution.py:306
  6.1 6.5 %collective-permute-start.1 = (bf16[192,128]{1,0:T(8,128)(2,1)S(1)}, bf16[192,128]{1,0:T(8,128)(2,1)S(1)}, u32[]{:S(2)}, u32[]{:S(2)}) collective-permute-start(bf16[192,128]{1,0:T(8,128)(2,1)S(1)} %get-tuple-element.26), channel_id=1, source_target_pairs={{0,3},{1,2},{2,1},{3,0},{4,7},{5,6},{6,5},{7,4},{8,11},{9,10},{10,... | collective-permute-start | bytes 147464 | tf_op jit(solution)/shard_map/ppermute | solution.py:306
  7.5 5.1 %collective-permute-start.2 = (bf16[192,128]{1,0:T(8,128)(2,1)S(1)}, bf16[192,128]{1,0:T(8,128)(2,1)S(1)}, u32[]{:S(2)}, u32[]{:S(2)}) collective-permute-start(bf16[192,128]{1,0:T(8,128)(2,1)S(1)} %get-tuple-element.28), channel_id=1, source_target_pairs={{0,1},{1,0},{2,3},{3,2},{4,5},{5,4},{6,7},{7,6},{8,9},{9,8},{10,11... | collective-permute-start | bytes 147464 | tf_op jit(solution)/shard_map/ppermute | solution.py:306
  7.7 11.0 %collective-permute-start.4 = (bf16[384,128]{1,0:T(8,128)(2,1)S(1)}, bf16[384,128]{1,0:T(8,128)(2,1)S(1)}, u32[]{:S(2)}, u32[]{:S(2)}) collective-permute-start(bf16[384,128]{1,0:T(8,128)(2,1)S(1)} %shard_map.91), channel_id=1, source_target_pairs={{0,2},{1,3},{2,0},{3,1},{4,6},{5,7},{6,4},{7,5},{8,10},{9,11},{10,... | collective-permute-start | bytes 294920 | tf_op jit(solution)/shard_map/ppermute | solution.py:306
  10.5 12.6 %collective-permute-start.5 = (bf16[384,128]{1,0:T(8,128)(2,1)S(1)}, bf16[384,128]{1,0:T(8,128)(2,1)S(1)}, u32[]{:S(2)}, u32[]{:S(2)}) collective-permute-start(bf16[384,128]{1,0:T(8,128)(2,1)S(1)} %shard_map.92), channel_id=1, source_target_pairs={{0,3},{1,2},{2,1},{3,0},{4,7},{5,6},{6,5},{7,4},{8,11},{9,10},{10,... | collective-permute-start | bytes 294920 | tf_op jit(solution)/shard_map/ppermute | solution.py:306
  12.8 11.0 %collective-permute-start.3 = (bf16[384,128]{1,0:T(8,128)(2,1)S(1)}, bf16[384,128]{1,0:T(8,128)(2,1)S(1)}, u32[]{:S(2)}, u32[]{:S(2)}) collective-permute-start(bf16[384,128]{1,0:T(8,128)(2,1)S(1)} %shard_map.89), channel_id=1, source_target_pairs={{0,1},{1,0},{2,3},{3,2},{4,5},{5,4},{6,7},{7,6},{8,9},{9,8},{10,11... | collective-permute-start | bytes 294920 | tf_op jit(solution)/shard_map/ppermute | solution.py:306
  15.6 10.4 %collective-permute-start.9 = (bf16[224,512]{1,0:T(8,128)(2,1)S(1)}, bf16[224,512]{1,0:T(8,128)(2,1)S(1)}, u32[]{:S(2)}, u32[]{:S(2)}) collective-permute-start(bf16[224,512]{1,0:T(8,128)(2,1)S(1)} %get-tuple-element.37), channel_id=1, source_target_pairs={{0,8},{4,12},{8,0},{12,4},{16,24},{20,28},{24,16},{28,20},{1,9},{5... | collective-permute-start | bytes 688136 | tf_op jit(solution)/shard_map/ppermute | solution.py:306
  17.1 10.9 %collective-permute-start.11 = (bf16[224,512]{1,0:T(8,128)(2,1)S(1)}, bf16[224,512]{1,0:T(8,128)(2,1)S(1)}, u32[]{:S(2)}, u32[]{:S(2)}) collective-permute-start(bf16[224,512]{1,0:T(8,128)(2,1)S(1)} %get-tuple-element.38), channel_id=1, source_target_pairs={{0,16},{4,20},{8,24},{12,28},{16,0},{20,4},{24,8},{28,12},{1,17},{... | collective-permute-start | bytes 688136 | tf_op jit(solution)/shard_map/ppermute | solution.py:306
  18.6 0.6 %copy-start = (bf16[384,128]{1,0:T(8,128)(2,1)}, bf16[384,128]{1,0:T(8,128)(2,1)S(1)}, u32[]{:S(2)}) copy-start(bf16[384,128]{1,0:T(8,128)(2,1)S(1)} %collective-permute-done.4.refs_2_) | copy-start | bytes 294916
  19.3 8.8 %collective-permute-start.6 = (bf16[224,512]{1,0:T(8,128)(2,1)S(1)}, bf16[224,512]{1,0:T(8,128)(2,1)S(1)}, u32[]{:S(2)}, u32[]{:S(2)}) collective-permute-start(bf16[224,512]{1,0:T(8,128)(2,1)S(1)} %get-tuple-element.35), channel_id=1, source_target_pairs={{0,24},{4,28},{8,16},{12,20},{16,8},{20,12},{24,0},{28,4},{1,25},{... | collective-permute-start | bytes 688136 | tf_op jit(solution)/shard_map/ppermute | solution.py:306
  23.1 0.6 %copy-start.2 = (bf16[384,128]{1,0:T(8,128)(2,1)}, bf16[384,128]{1,0:T(8,128)(2,1)S(1)}, u32[]{:S(2)}) copy-start(bf16[384,128]{1,0:T(8,128)(2,1)S(1)} %collective-permute-done.5.refs_3_) | copy-start | bytes 294916
  23.7 4.8 %collective-permute-start.8 = (bf16[224,512]{1,0:T(8,128)(2,1)S(1)}, bf16[224,512]{1,0:T(8,128)(2,1)S(1)}, u32[]{:S(2)}, u32[]{:S(2)}) collective-permute-start(bf16[224,512]{1,0:T(8,128)(2,1)S(1)} %get-tuple-element.29.refs_1_.mine_ref.refs_0_), channel_id=1, source_target_pairs={{0,4},{4,0},{8,12},{12,8},{16,20},{20,16},{24,28},{28,24},{1,5},{5... | collective-permute-start | bytes 688136 | tf_op jit(solution)/shard_map/ppermute | solution.py:306
  23.8 0.9 %copy-start.1 = (bf16[384,128]{1,0:T(8,128)(2,1)S(1)}, bf16[384,128]{1,0:T(8,128)(2,1)}, u32[]{:S(2)}) copy-start(bf16[384,128]{1,0:T(8,128)(2,1)} %copy-done) | copy-start | bytes 294916
  24.6 0.9 %copy-start.3 = (bf16[384,128]{1,0:T(8,128)(2,1)S(1)}, bf16[384,128]{1,0:T(8,128)(2,1)}, u32[]{:S(2)}) copy-start(bf16[384,128]{1,0:T(8,128)(2,1)} %copy-done.2) | copy-start | bytes 294916
  26.1 2.5 %collective-permute-start.10 = (bf16[224,512]{1,0:T(8,128)(2,1)S(1)}, bf16[224,512]{1,0:T(8,128)(2,1)S(1)}, u32[]{:S(2)}, u32[]{:S(2)}) collective-permute-start(bf16[224,512]{1,0:T(8,128)(2,1)S(1)} %collective-permute-done.9.refs_2_), channel_id=1, source_target_pairs={{0,4},{4,0},{8,12},{12,8},{16,20},{20,16},{24,28},{28,24},{1,5},{5... | collective-permute-start | bytes 688136 | tf_op jit(solution)/shard_map/ppermute | solution.py:306
  28.1 1.5 %collective-permute-start.12 = (bf16[224,512]{1,0:T(8,128)(2,1)S(1)}, bf16[224,512]{1,0:T(8,128)(2,1)S(1)}, u32[]{:S(2)}, u32[]{:S(2)}) collective-permute-start(bf16[224,512]{1,0:T(8,128)(2,1)S(1)} %collective-permute-done.11.refs_4_), channel_id=1, source_target_pairs={{0,4},{4,0},{8,12},{12,8},{16,20},{20,16},{24,28},{28,24},{1,5},{5... | collective-permute-start | bytes 688136 | tf_op jit(solution)/shard_map/ppermute | solution.py:306
  28.1 2.0 %collective-permute-start.7 = (bf16[224,512]{1,0:T(8,128)(2,1)S(1)}, bf16[224,512]{1,0:T(8,128)(2,1)S(1)}, u32[]{:S(2)}, u32[]{:S(2)}) collective-permute-start(bf16[224,512]{1,0:T(8,128)(2,1)S(1)} %shard_map.94.refs_0_), channel_id=1, source_target_pairs={{0,4},{4,0},{8,12},{12,8},{16,20},{20,16},{24,28},{28,24},{1,5},{5... | collective-permute-start | bytes 688136 | tf_op jit(solution)/shard_map/ppermute | solution.py:306
